TPU v7x, 256 devices: a whole 4x4x8 slice. The times are simulated.
256 devices in a mesh: rep: 8 (over z_lo, core), fsdp: 32 (over x, z_hi, y).
Axes of the slice: x: 4, y: 4, z: 8 (z_hi: 2, z_lo: 4; z = z_hi * 4 + z_lo), core: 2. Of those that a mesh axis runs over, the one named last changes fastest.
Arguments:
- activations: bfloat16 [131072, 5120], P(('rep', 'fsdp')), may hold values from -6 to 6
- cotangents: bfloat16 [131072, 1024], P(('rep', 'fsdp')), may hold values from -0.01171875 to 0.01171875
- weights: bfloat16 [5120, 1024], P('fsdp'), may hold values from -0.078125 to 0.078125
- momentum: float32 [8, 5120, 1024], P('rep', 'fsdp'), may hold values from -6 to 6
- positions: int32 [8, 5120, 16, 8], P('rep', 'fsdp'), may hold values from 0 to 63, as said below
Outputs:
- new_momentum: float32 [8, 5120, 1024], P('rep', 'fsdp')
- new_weights: bfloat16 [5120, 1024], P('fsdp')
- new_keys: bfloat16 [131072, 1024], P(('rep', 'fsdp'))
Inputs may be any that keep to these rules, and one draw needn't show every extreme that they name: The 8 positions of one span are distinct.
All inputs are finite; a program needn't handle non-finite values.
Results may differ from a plain program's by a relative error of at most 0.01.
Values may be sent and summed in bfloat16 or wider, within the bound.
A program may use at most 128 MiB of HBM per device.

v0:
```python
import math

import jax
import jax.numpy as jnp
from jax import lax
from jax.sharding import PartitionSpec as P


def dct_table():
    freq = lax.broadcasted_iota(jnp.float32, (64, 64), 0)
    place = lax.broadcasted_iota(jnp.float32, (64, 64), 1)
    weight = jnp.where(freq == 0, math.sqrt(1.0 / 64), math.sqrt(2.0 / 64))
    return weight * jnp.cos(math.pi * (2.0 * place + 1.0) * freq / 128.0)


def on_device(activations, cotangents, weights, momentum, positions):
    table = dct_table()
    own_rows = weights.shape[0]
    width = weights.shape[1]
    groups = lax.axis_size("rep")
    slots = lax.broadcasted_iota(jnp.int32, (1, 1, 1, 64), 3)
    columns = activations
    grad = lax.psum_scatter(
        lax.dot_general(
            columns, cotangents, (((0,), (0,)), ((), ())), preferred_element_type=jnp.float32
        ).astype(jnp.bfloat16),
        "fsdp",
        scatter_dimension=0,
        tiled=True,
    ).astype(jnp.float32)
    moment = 0.9 * momentum[0] + grad
    spans = moment.reshape(own_rows, width // 64, 64)
    coeffs = jnp.einsum("ijn,kn->ijk", spans, table, precision=lax.Precision.HIGHEST)
    own_pos = positions[0]
    onehot = (own_pos[..., None] == slots).astype(jnp.float32)
    kept = jnp.sum(onehot * coeffs[:, :, None, :], axis=3)
    all_kept, all_pos = (
        lax.all_gather(kept[None], "rep", axis=0, tiled=True),
        lax.all_gather(own_pos[None], "rep", axis=0, tiled=True),
    )
    sparse = jnp.sum(kept[..., None] * onehot, axis=2)
    sent = jnp.einsum("ijk,kn->ijn", sparse, table, precision=lax.Precision.HIGHEST)
    new_momentum = (moment - sent.reshape(own_rows, width))[None]
    every_hot = (all_pos[..., None] == slots[None]).astype(jnp.float32)
    every_sparse = jnp.einsum(
        "rijt,rijtk->rijk", all_kept, every_hot, precision=lax.Precision.HIGHEST
    )
    decoded = jnp.einsum("rijk,kn->rijn", every_sparse, table, precision=lax.Precision.HIGHEST)
    update = jnp.sum(decoded, axis=0)
    update = update.reshape(own_rows, width) / groups
    new_weights = (weights.astype(jnp.float32) - 0.03 * update).astype(jnp.bfloat16)
    columns = activations
    keys = jnp.dot(
        columns,
        lax.all_gather(new_weights, "fsdp", axis=0, tiled=True),
        preferred_element_type=jnp.float32,
    )
    return (new_momentum, new_weights, keys.astype(jnp.bfloat16))


def solution(mesh):
    placed = (
        P(("rep", "fsdp"), None),
        P(("rep", "fsdp"), None),
        P("fsdp", None),
        P("rep", "fsdp", None),
        P("rep", "fsdp", None, None),
    )
    return jax.shard_map(
        on_device,
        mesh=mesh,
        in_specs=placed,
        out_specs=(P("rep", "fsdp", None), P("fsdp", None), P(("rep", "fsdp"), None)),
        check_vma=False,
    )
```

profile of v0, /device:TPU:1, one launch (start us, length us, event | category | flops | bytes accessed | tf_op | source)
XLA Modules:
  0.0 585.1 jit_solution(4129972238628798171)
XLA Ops:
  7.2 0.0 copy-start
  7.2 0.0 reduce-scatter.2.cloned.1.call-start
  7.2 1.2 copy-done
  8.4 10.9 %convolution_convert_fusion = bf16[5120,1024]{1,0:T(8,128)(2,1)} fusion(bf16[512,5120]{1,0:T(8,128)(2,1)} %param.5, bf16[512,1024]{1,0:T(8,128)(2,1)S(1)} %copy-done), kind=kOutput, calls=%fused_computation.2 | convolution fusion | flops 5373952000 | bytes 16777216 | tf_op jit(solution)/shard_map/dot_general | solution.py:24
  19.3 0.0 copy-start.1
  19.3 0.0 copy-start.2
  19.3 0.0 reduce-scatter.2.cloned.1.call-update
  19.3 0.0 all-gather.3.cloned.1.call-start
  19.4 0.8 copy-done.1
  20.2 19.3 %all_gather.10 = s32[8,160,16,8]{1,3,2,0:T(8,128)S(1)} all-gather(s32[1,160,16,8]{1,3,2,0:T(8,128)S(1)} %copy-done.1), channel_id=1, replica_groups=mesh['rep'=8,'fsdp'=32] {'rep'}, dimensions={0}, use_global_device_ids=true | all-gather | bytes 737280 | tf_op jit(solution)/shard_map/all_gather | solution.py:39
  39.5 262.4 %reduce-scatter.2.cloned.1.call-done = bf16[160,1024]{1,0:T(8,128)(2,1)} async-done(((bf16[5120,1024]{1,0:T(8,128)(2,1)}), bf16[160,1024]{1,0:T(8,128)(2,1)}) %reduce-scatter.2.cloned.1.call-update) | async-done | bytes 327696 | tf_op jit(solution)/shard_map/reduce_scatter | solution.py:23
  301.8 0.0 copy-done.2
  301.8 1.1 bitcast_add_fusion
  302.9 1.3 copy.44
  304.2 2.4 fusion.4
  306.6 3.2 select_reduce_fusion.2
  309.9 1.2 copy.34
  311.1 48.7 %all-gather = f32[1280,16,8]{1,2,0:T(8,128)} all-gather(f32[160,16,8]{1,2,0:T(8,128)S(1)} %copy.34), channel_id=2, replica_groups=mesh['rep'=8,'fsdp'=32] {'rep'}, dimensions={0}, use_global_device_ids=true | all-gather | bytes 737280 | tf_op jit(solution)/shard_map/all_gather | solution.py:38
  359.8 4.8 copy.48
  364.6 17.5 %select_reduce_fusion = f32[8,160,16,64]{1,3,2,0:T(8,128)} fusion(f32[8,160,16,8]{1,3,2,0:T(8,128)} %copy.48, s32[8,160,16,8]{1,3,2,0:T(8,128)S(1)} %all_gather.10), kind=kLoop, calls=%fused_computation | loop fusion | flops 30146560 | bytes 6553600 | tf_op jit(solution)/shard_map/rijt,rijtk->rijk/dot_general | solution.py:45
  382.1 11.3 %convolution_reduce_fusion = f32[160,16,64]{0,2,1:T(8,128)S(1)} fusion(f32[8,160,16,64]{1,3,2,0:T(8,128)} %select_reduce_fusion, f32[64]{0:T(128)S(1)} %get-tuple-element.16, f32[64]{0:T(128)S(1)} %multiply_add_fusion, f32[64]{0:T(128)S(1)} %get-tuple-element.15), kind=kOutput, calls=%fused_computation.6 | convolution fusion | flops 1007792128 | bytes 5899008 | tf_op jit(solution)/shard_map/rijk,kn->rijn/dot_general | solution.py:48
  393.4 0.1 broadcast_multiply_fusion
  393.6 0.3 copy.47
  393.9 1.8 subtract_convert_fusion
  395.6 0.0 all-gather.3.cloned.1.call-update
  395.7 2.5 select_reduce_fusion.1
  398.1 1.3 fusion.2
  399.4 0.3 copy.46
  399.7 0.9 subtract_bitcast_fusion
  400.6 166.2 %all-gather.3.cloned.1.call-done = bf16[5120,1024]{1,0:T(8,128)(2,1)} async-done(((bf16[160,1024]{1,0:T(8,128)(2,1)}), bf16[5120,1024]{1,0:T(8,128)(2,1)}) %all-gather.3.cloned.1.call-update) | async-done | bytes 10485776 | tf_op jit(solution)/shard_map/all_gather | solution.py:55
  566.8 10.1 %fusion = bf16[512,1024]{0,1:T(8,128)(2,1)S(1)} fusion(bf16[5120,1024]{1,0:T(8,128)(2,1)} %all-gather.3.cloned.1.call-done, bf16[512,5120]{1,0:T(8,128)(2,1)} %param.5), kind=kOutput, calls=%fused_computation.8 | convolution fusion | flops 5369233408 | bytes 16777216 | tf_op jit(solution)/shard_map/dot_general | solution.py:53
  576.9 1.3 copy.36
  (2 shorter events, 0.0 us)
Async XLA Ops:
  7.2 1.2 copy-start
  7.2 294.6 %reduce-scatter.2.cloned.1.call-start = ((), (), s32[]{:S(2)}) async-start(), calls=%async_computation.1 | async-start | bytes 10813440 | tf_op jit(solution)/shard_map/reduce_scatter | solution.py:23
  19.3 0.9 copy-start.1
  19.3 282.5 %copy-start.2 = (f32[1,160,1024]{2,1,0:T(8,128)S(1)}, f32[1,160,1024]{2,1,0:T(8,128)}, u32[]{:S(2)}) copy-start(f32[1,160,1024]{2,1,0:T(8,128)} %param.8) | copy-start | bytes 1966084
  19.3 547.5 %all-gather.3.cloned.1.call-start = ((), (), s32[]{:S(2)}) async-start(), calls=%async_computation.2 | async-start | bytes 10813440 | tf_op jit(solution)/shard_map/all_gather | solution.py:55
Sparse Core Ops, SparseCore 0:
  19.4 282.3 reduce-scatter.1
  395.8 170.9 all-gather.2
where the time goes:
time: 585 us
  waiting for transfers between devices  429 us (73%)
  blocking collectives  68 us (12%)
  matrix products  36 us (6%)
  other arithmetic  27 us (5%)
  between operations  14.1 us (2%)
  local copies, waits for them, and re-layouts  11.2 us (2%)
    reduce_scatter x1, waiting for transfers between devices, on_device(): lax.psum_scatter(lax.dot_general(columns, cotangents, (((0,), (0,)), ((),...  262 us
    all_gather x1, waiting for transfers between devices, on_device(): lax.all_gather(new_weights, 'fsdp', axis=0, tiled=True)  166 us
    all_gather x1, blocking collectives, on_device(): lax.all_gather(kept[None], 'rep', axis=0, tiled=True)  48.7 us
    all_gather x1, blocking collectives, on_device(): lax.all_gather(own_pos[None], 'rep', axis=0, tiled=True)  19.3 us
    dot_general x1, other arithmetic, on_device(): jnp.einsum('rijt,rijtk->rijk', all_kept, every_hot, precision=lax.Precisi...  17.5 us
  transfers between devices with their start and end apart: 2, of which 2 were waited for; matrix products, arithmetic and copies ran while one was open for 1% of the time, Pallas kernels for 0%

commit v1 on v0

v1 whole, which is shorter than its diff:
```python
import functools
import math

import jax
import jax.numpy as jnp
import numpy as np
from jax import lax
from jax.experimental import pallas as pl
from jax.experimental.pallas import tpu as pltpu
from jax.sharding import PartitionSpec as P

MESH = pl.DeviceIdType.MESH
BF = jnp.bfloat16
F32 = jnp.float32
N_COPIES = 128


def transforms():
    k = np.arange(64, dtype=np.float64)[:, None]
    n = np.arange(64, dtype=np.float64)[None, :]
    table = np.where(k == 0, math.sqrt(1.0 / 64), math.sqrt(2.0 / 64)) * np.cos(math.pi * (2 * n + 1) * k / 128)
    back = np.kron(np.eye(4), table).astype(np.float32)
    high = back.astype(jnp.bfloat16)
    low = (back - high.astype(np.float32)).astype(jnp.bfloat16)
    return np.stack([high.T, low.T, high, low])


def dot3(value, high, low):
    top = value.astype(BF)
    rest = (value - top.astype(F32)).astype(BF)
    dot = functools.partial(jnp.dot, preferred_element_type=F32)
    return dot(top, high) + (dot(rest, high) + dot(top, low))


def kernel(
    acts, cots, weights, momentum, pos, dct,
    new_mom, new_w, keys,
    sib_acts, part, hop, plus, minus, hop2, plus2, minus2, cross, cross_in,
    mask, sent, sib_in, pair, pair_in, gathered, total, far_keys,
    send_sems, recv_sems,
):
    rep, fsdp = lax.axis_index("rep"), lax.axis_index("fsdp")
    x, zh, y = fsdp // 8, (fsdp // 4) % 2, fsdp % 4
    zl, core = rep // 2, rep % 2
    z = zh * 4 + zl
    me = (x, y)

    def device(dx=0, dy=0, dz=0, flip=False):
        nz = (z + dz) % 8
        return (
            (nz % 4) * 2 + ((1 - core) if flip else core),
            ((x + dx) % 4) * 8 + (nz // 4) * 4 + (y + dy) % 4,
        )

    def along(axis, step):
        return device(dx=step) if axis == 0 else device(dy=step)

    used = [0]

    def send(src, dst, target):
        slot = used[0]
        used[0] += 1
        copy = pltpu.make_async_remote_copy(
            src_ref=src, dst_ref=dst, send_sem=send_sems.at[slot], recv_sem=recv_sems.at[slot],
            device_id=target, device_id_type=MESH,
        )
        copy.start()
        return copy

    sent_copies = []

    def push(src, dst, target):
        copy = send(src, dst, target)
        sent_copies.append(copy)
        return copy

    peers = [along(0, 1), along(0, -1), along(1, 1), along(1, -1), device(flip=True)]
    peers += [device(dz=d) for d in range(1, 8)]
    barrier = pltpu.get_barrier_semaphore()
    for peer in peers:
        pl.semaphore_signal(barrier, inc=1, device_id=peer, device_id_type=MESH)
    pl.semaphore_wait(barrier, len(peers))

    def multiply(half, ux):
        unit = ux * 2 + half
        columns = acts[:, pl.ds(pl.multiple_of(unit * 640, 128), 640)]
        out = lax.dot_general(columns, cots[...], (((0,), (0,)), ((), ())), preferred_element_type=F32).astype(BF)
        for uy in range(4):
            part[0, half, ux, uy] = out[uy * 160 : uy * 160 + 80]
            part[1, half, uy, ux] = out[uy * 160 + 80 : uy * 160 + 160]

    def chunk(s, half, j, h):
        return part.at[s, half, j, pl.ds(2 * h, 2)]

    class First:
        def __init__(self, s, turn, half):
            self.s, self.turn, self.half, self.p = s, turn, half, me[s]

        def open(self):
            s, turn, half, p = self.s, self.turn, self.half, self.p
            across = (p + 2) % 4
            self.up1 = push(chunk(s, half, across, 0), hop.at[s, turn, 0], along(s, 1))
            self.down1 = push(chunk(s, half, across, 1), hop.at[s, turn, 1], along(s, -1))

        def open2(self):
            s, turn, half, p = self.s, self.turn, self.half, self.p
            after, before = (p + 1) % 4, (p + 3) % 4
            self.up2 = push(chunk(s, half, after, 1), plus.at[s, turn, pl.ds(2, 2)], along(s, 1))
            self.down2 = push(chunk(s, half, before, 0), minus.at[s, turn, pl.ds(0, 2)], along(s, -1))

        def relay(self):
            s, turn, half, p = self.s, self.turn, self.half, self.p
            after, before = (p + 1) % 4, (p + 3) % 4
            self.up1.wait_recv()
            ref = chunk(s, half, after, 0)
            ref[...] = (ref[...].astype(F32) + hop[s, turn, 0].astype(F32)).astype(BF)
            self.up3 = push(ref, plus.at[s, turn, pl.ds(0, 2)], along(s, 1))
            self.down1.wait_recv()
            ref = chunk(s, half, before, 1)
            ref[...] = (ref[...].astype(F32) + hop[s, turn, 1].astype(F32)).astype(BF)
            self.down3 = push(ref, minus.at[s, turn, pl.ds(2, 2)], along(s, -1))

        def close(self):
            s, turn, half, p = self.s, self.turn, self.half, self.p
            for copy in (self.up2, self.down2, self.up3, self.down3):
                copy.wait_recv()
            ref = part.at[s, half, p]
            ref[...] = (
                ref[...].astype(F32) + plus[s, turn].astype(F32) + minus[s, turn].astype(F32)
            ).astype(BF)

    class Second:
        def __init__(self, s, turn, half):
            self.s, self.turn, self.half, self.p1, self.p = s, turn, half, me[s], me[1 - s]

        def block(self, j, h):
            return part.at[self.s, self.half, self.p1, j, :, pl.ds(512 * h, 512)]

        def open(self):
            s, turn, p = self.s, self.turn, self.p
            across, after, before = (p + 2) % 4, (p + 1) % 4, (p + 3) % 4
            ax = 1 - s
            self.up1 = push(self.block(across, 0), hop2.at[s, turn, 0], along(ax, 1))
            self.down1 = push(self.block(across, 1), hop2.at[s, turn, 1], along(ax, -1))
            self.up2 = push(self.block(after, 1), plus2.at[s, turn, 1], along(ax, 1))
            self.down2 = push(self.block(before, 0), minus2.at[s, turn, 0], along(ax, -1))

        def relay(self):
            s, turn, p = self.s, self.turn, self.p
            after, before = (p + 1) % 4, (p + 3) % 4
            ax = 1 - s
            self.up1.wait_recv()
            ref = self.block(after, 0)
            ref[...] = (ref[...].astype(F32) + hop2[s, turn, 0].astype(F32)).astype(BF)
            self.up3 = push(ref, plus2.at[s, turn, 0], along(ax, 1))
            self.down1.wait_recv()
            ref = self.block(before, 1)
            ref[...] = (ref[...].astype(F32) + hop2[s, turn, 1].astype(F32)).astype(BF)
            self.down3 = push(ref, minus2.at[s, turn, 1], along(ax, -1))

        def arrive(self):
            for copy in (self.up2, self.down2, self.up3, self.down3):
                copy.wait_recv()

        def value(self, g):
            s, turn = self.s, self.turn
            h, lanes = g // 2, slice(g % 2 * 256, g % 2 * 256 + 256)
            return (
                part[s, self.half, self.p1, self.p, :, g * 256 : g * 256 + 256].astype(F32)
                + plus2[s, turn, h, :, lanes].astype(F32)
                + minus2[s, turn, h, :, lanes].astype(F32)
            )

    other = 1 - zh
    firsts = [[First(s, 0, other), First(s, 1, zh)] for s in range(2)]
    seconds = [[Second(s, 0, other), Second(s, 1, zh)] for s in range(2)]

    multiply(other, (x + 2) % 4)
    firsts[0][0].open()
    multiply(other, (x + 1) % 4)
    multiply(other, (x + 3) % 4)
    firsts[0][0].open2()
    multiply(other, x)
    firsts[1][0].open()
    firsts[1][0].open2()
    pl.loop(0, 4)(lambda k: multiply(zh, (x + 2 + k) % 4))

    firsts[0][0].relay()
    firsts[0][1].open()
    firsts[0][1].open2()
    firsts[1][0].relay()
    firsts[1][1].open()
    firsts[1][1].open2()

    acts_copy = push(acts, sib_acts, device(flip=True))
    places = pos[...].astype(F32).astype(BF)
    lane = lax.broadcasted_iota(jnp.int32, (128, 1024), 1)
    row = lax.broadcasted_iota(jnp.int32, (128, 1024), 0)
    slot = (lax.broadcasted_iota(jnp.int32, (160, 1024), 1) % 64).astype(F32)
    mask[...] = jnp.zeros_like(mask)
    for t in range(8):
        pick = (row == lane // 64 * 8 + t).astype(F32).astype(BF)
        at = lax.dot_general(places, pick, (((0,), (0,)), ((), ())), preferred_element_type=F32)
        mask[...] += (at == slot).astype(F32)

    firsts[0][0].close()
    seconds[0][0].open()
    firsts[1][0].close()
    seconds[1][0].open()
    seconds[0][0].relay()
    firsts[0][1].relay()
    seconds[1][0].relay()
    firsts[1][1].relay()

    crossing = []
    for s in range(2):
        seconds[s][0].arrive()
        for g in range(4):
            cross[s, :, g * 256 : g * 256 + 256] = seconds[s][0].value(g).astype(BF)
        crossing.append(push(cross.at[s], cross_in.at[s], device(dz=4)))

    for s in range(2):
        firsts[s][1].close()
        seconds[s][1].open()
    for s in range(2):
        seconds[s][1].relay()

    sib_copies = []
    for s in range(2):
        seconds[s][1].arrive()
        crossing[s].wait_recv()
        rows = slice(s * 80, s * 80 + 80)
        for g in range(4):
            cols = slice(g * 256, g * 256 + 256)
            grad = seconds[s][1].value(g) + cross_in[s, :, cols].astype(F32)
            moment = 0.9 * momentum[rows, cols] + grad
            sparse = dot3(moment, dct[0], dct[1]) * mask[rows, cols]
            decoded = dot3(sparse, dct[2], dct[3])
            new_mom[rows, cols] = moment - decoded
            decoded = decoded.astype(BF)
            sent[s, 2 * g] = decoded[:, :128]
            sent[s, 2 * g + 1] = decoded[:, 128:]
        sib_copies.append(push(sent.at[s, pl.ds(4 * (1 - core), 4)], sib_in.at[s], device(flip=True)))

    pair_copies = []
    for s in range(2):
        sib_copies[s].wait_recv()
        for k in range(4):
            pair[s, k] = (sent[s, 4 * core + k].astype(F32) + sib_in[s, k].astype(F32)).astype(BF)
        copies = []
        for d in range(1, 4):
            peer = (zl + d) % 4
            copies.append(push(pair.at[s, peer], pair_in.at[s, d - 1], (peer * 2 + core, fsdp)))
        pair_copies.append(copies)

    own = 2 * x + zh
    q_me, lanes_me = zl // 2, pl.ds(pl.multiple_of((zl % 2) * 128, 128), 128)
    spread = []
    for s in range(2):
        for copy in pair_copies[s]:
            copy.wait_recv()
        update = pair[s, zl].astype(F32)
        for d in range(3):
            update = update + pair_in[s, d].astype(F32)
        old = weights[s * 80 : s * 80 + 80, pl.ds(pl.multiple_of((core * 4 + zl) * 128, 128), 128)]
        gathered[q_me, own, y, s, :, lanes_me] = (old.astype(F32) - (0.03 / 8) * update).astype(BF)
        block = gathered.at[q_me, own, y, s, :, lanes_me]
        spread.append([push(block, block, device(dz=d)) for d in range(1, 8)])

    near = []
    for s in range(2):
        for copy in spread[s]:
            copy.wait_recv()
        block = gathered.at[:, pl.ds(2 * x, 2), y, s]
        near.append([push(block, block, along(s, 1)), push(block, block, along(s, -1))])
        for q in range(2):
            lanes = pl.ds(pl.multiple_of(core * 512 + q * 256, 256), 256)
            new_w[s * 80 : s * 80 + 80, lanes] = gathered[q, own, y, s]
            mine = gathered.at[q, own, y, s]
            near[s].append(push(mine, new_w.at[pl.ds(s * 80, 80), lanes], device(flip=True)))

    for s in range(2):
        up, down = near[s][:2]
        up.wait_recv()
        down.wait_recv()
        spots = []
        for h, step in ((0, -1), (1, 1)):
            if s == 0:
                spots.append(gathered.at[:, 2 * ((x + step) % 4) + h, y, s])
            else:
                spots.append(gathered.at[:, 2 * x + h, (y + step) % 4, s])
        near[s].append(push(spots[0], spots[0], along(s, 1)))
        near[s].append(push(spots[1], spots[1], along(s, -1)))

    far = [[None, None], [None, None]]
    for s in range(2):
        for copy in near[s][4:]:
            copy.wait_recv()
        for q in range(2):
            if s == 0:
                block = gathered.at[q, :, y, s]
            else:
                block = gathered.at[q, pl.ds(2 * x, 2), :, s]
            far[s][q] = [push(block, block, along(1 - s, 1)), push(block, block, along(1 - s, -1))]
    for q in range(2):
        for s in range(2):
            for copy in far[s][q]:
                copy.wait_recv()
            spots = []
            for h, step in ((0, -1), (1, 1)):
                if s == 0:
                    spots.append(gathered.at[q, pl.ds(4 * h, 4), (y + step) % 4, s])
                else:
                    spots.append(gathered.at[q, 2 * ((x + step) % 4) + h, :, s])
            far[s][q] = [
                push(spots[0], spots[0], along(1 - s, 1)),
                push(spots[1], spots[1], along(1 - s, -1)),
            ]

    acts_copy.wait_recv()
    back = []
    for q in range(2):
        for s in range(2):
            for copy in far[s][q]:
                copy.wait_recv()
        total[...] = jnp.zeros_like(total)

        @pl.loop(0, 4)
        def _(k):
            rows = gathered[q, pl.ds(2 * k, 2)].reshape(1280, 256)
            lanes = pl.ds(pl.multiple_of(k * 1280, 128), 1280)
            total[0] += jnp.dot(sib_acts[:, lanes], rows, preferred_element_type=F32)
            total[1] += jnp.dot(acts[:, lanes], rows, preferred_element_type=F32)

        lanes = pl.ds(pl.multiple_of(core * 512 + q * 256, 256), 256)
        far_keys[q] = total[0].astype(BF)
        back.append(push(far_keys.at[q], keys.at[:, lanes], device(flip=True)))
        keys[:, lanes] = total[1].astype(BF)

    for copy in near[0][2:4] + near[1][2:4] + back:
        copy.wait_recv()
    for copy in sent_copies:
        copy.wait_send()


def on_device(activations, cotangents, weights, momentum, positions):
    vmem = pl.BlockSpec(memory_space=pltpu.VMEM)
    pos = positions[0].transpose(1, 2, 0).reshape(128, 160)
    dma = pltpu.SemaphoreType.DMA((N_COPIES,))
    new_mom, new_w, keys = pl.pallas_call(
        kernel,
        name="step",
        out_shape=(
            jax.ShapeDtypeStruct((160, 1024), F32),
            jax.ShapeDtypeStruct((160, 1024), BF),
            jax.ShapeDtypeStruct((512, 1024), BF),
        ),
        in_specs=[vmem] * 6,
        out_specs=(vmem, vmem, vmem),
        scratch_shapes=[
            pltpu.VMEM((512, 5120), BF),
            pltpu.VMEM((2, 2, 4, 4, 80, 1024), BF),
            pltpu.VMEM((2, 2, 2, 2, 80, 1024), BF),
            pltpu.VMEM((2, 2, 4, 80, 1024), BF),
            pltpu.VMEM((2, 2, 4, 80, 1024), BF),
            pltpu.VMEM((2, 2, 2, 80, 512), BF),
            pltpu.VMEM((2, 2, 2, 80, 512), BF),
            pltpu.VMEM((2, 2, 2, 80, 512), BF),
            pltpu.VMEM((2, 80, 1024), BF),
            pltpu.VMEM((2, 80, 1024), BF),
            pltpu.VMEM((160, 1024), F32),
            pltpu.VMEM((2, 8, 80, 128), BF),
            pltpu.VMEM((2, 4, 80, 128), BF),
            pltpu.VMEM((2, 4, 80, 128), BF),
            pltpu.VMEM((2, 3, 80, 128), BF),
            pltpu.VMEM((2, 8, 4, 2, 80, 256), BF),
            pltpu.VMEM((2, 512, 256), F32),
            pltpu.VMEM((2, 512, 256), BF),
            dma,
            dma,
        ],
        compiler_params=pltpu.CompilerParams(
            collective_id=0, has_side_effects=True, vmem_limit_bytes=60 * 2**20
        ),
    )(activations, cotangents, weights, momentum[0], pos, jnp.asarray(transforms()))
    return new_mom[None], new_w, keys


def solution(mesh):
    placed = (
        P(("rep", "fsdp"), None),
        P(("rep", "fsdp"), None),
        P("fsdp", None),
        P("rep", "fsdp", None),
        P("rep", "fsdp", None, None),
    )
    return jax.shard_map(
        on_device,
        mesh=mesh,
        in_specs=placed,
        out_specs=(P("rep", "fsdp", None), P("fsdp", None), P(("rep", "fsdp"), None)),
        check_vma=False,
    )
```

time: 585 us -> 138 us (0.24)
  waiting for transfers between devices: 429 us -> 0 us
  Pallas kernels: 0 us -> 132 us
  blocking collectives: 68 us -> 0 us
  matrix products: 36 us -> 0 us
  other arithmetic: 27 us -> 0 us
  between operations: 14.1 us -> 0.64 us
    reduce_scatter x1 -> x0, waiting for transfers between devices: 262 us -> none  [on_device(): lax.psum_scatter(lax.dot_general(columns, cotangents, (((0,), (0,)), ((),...]
    all_gather x1 -> x0, waiting for transfers between devices: 166 us -> none  [on_device(): lax.all_gather(new_weights, 'fsdp', axis=0, tiled=True)]
    pallas_call x0 -> x1, Pallas kernels: none -> 132 us  [on_device(): pl.pallas_call(kernel, name='step', out_shape=(jax.ShapeDtypeStruct((160,...]
    all_gather x2 -> x0, blocking collectives: 68 us -> none  [the longest x1 48.7 us: on_device(): lax.all_gather(kept[None], 'rep', axis=0, tiled=True)]
    dot_general x5 -> x0, matrix products: 36 us -> none  [the longest x1 11.3 us: on_device(): jnp.einsum('rijk,kn->rijn', every_sparse, table, precision=lax.Precision....]
    dot_general x1 -> x0, other arithmetic: 17.5 us -> none  [on_device(): jnp.einsum('rijt,rijtk->rijk', all_kept, every_hot, precision=lax.Precisi...]
  transfers between devices with their start and end apart: 2 -> 0, of which waited for: 2 -> 0; matrix products, arithmetic and copies ran while one was open for 1% -> 0% of each run, Pallas kernels for 0% -> 0%
where the time goes in v1:
time: 138 us
  Pallas kernels  132 us (96%)
  local copies, waits for them, and re-layouts  5.96 us (4%)
    pallas_call x1, Pallas kernels, on_device(): pl.pallas_call(kernel, name='step', out_shape=(jax.ShapeDtypeStruct((160,...  132 us
    unnamed x3, local copies, waits for them, and re-layouts  5.96 us

profile of v1, /device:TPU:1, one launch (start us, length us, event | category | flops | bytes accessed | tf_op | source)
XLA Modules:
  0.0 138.2 jit_solution(3705749551542047545)
XLA Ops:
  0.6 131.6 %step.1 = (f32[160,1024]{1,0:T(8,128)}, bf16[160,1024]{1,0:T(8,128)(2,1)}, bf16[512,1024]{1,0:T(8,128)(2,1)}) custom-call(bf16[512,5120]{1,0:T(8,128)(2,1)} %acts.1, bf16[512,1024]{1,0:T(8,128)(2,1)} %cots.1, bf16[160,1024]{1,0:T(8,128)(2,1)} %weights.1, f32[160,1024]{1,0:T(8,128)} %bitcast.8, s32[128,160]{1,0:T(8,128)} %bitcast.9, ...), custom_call_target="tpu_custom_call" | custom-call | tf_op jit(solution)/shard_map/step/pallas_call | solution.py:350
  132.2 2.0 %copy.12 = f32[1,160,1024]{2,1,0:T(8,128)} copy(f32[1,160,1024]{2,1,0:T(8,128)} %bitcast.7) | data formatting | bytes 1310720
  134.2 1.7 %copy.13 = bf16[160,1024]{1,0:T(8,128)(2,1)} copy(bf16[160,1024]{1,0:T(8,128)(2,1)} %get-tuple-element.13) | data formatting | bytes 655360
  135.9 2.3 %copy.14 = bf16[512,1024]{1,0:T(8,128)(2,1)} copy(bf16[512,1024]{1,0:T(8,128)(2,1)} %get-tuple-element.14) | data formatting | bytes 2097152

commit v2 on v0

v2 whole, which is shorter than its diff:
```python
import functools
import math

import jax
import jax.numpy as jnp
import numpy as np
from jax import lax
from jax.experimental import pallas as pl
from jax.experimental.pallas import tpu as pltpu
from jax.sharding import PartitionSpec as P

MESH = pl.DeviceIdType.MESH
BF = jnp.bfloat16
F32 = jnp.float32
N_COPIES = 192
WIDE = 512


def transforms():
    k = np.arange(64, dtype=np.float64)[:, None]
    n = np.arange(64, dtype=np.float64)[None, :]
    table = np.where(k == 0, math.sqrt(1.0 / 64), math.sqrt(2.0 / 64)) * np.cos(math.pi * (2 * n + 1) * k / 128)
    back = np.kron(np.eye(4), table).astype(np.float32)
    high = back.astype(jnp.bfloat16)
    low = (back - high.astype(np.float32)).astype(jnp.bfloat16)
    return np.stack([high.T, low.T, high, low])


def dot3(value, high, low):
    top = value.astype(BF)
    rest = (value - top.astype(F32)).astype(BF)
    dot = functools.partial(jnp.dot, preferred_element_type=F32)
    return dot(top, high) + (dot(rest, high) + dot(top, low))


def kernel(
    acts_in, cots_in, weights_in, momentum_in, pos_in, dct_in,
    new_mom, new_w, keys,
    acts, cots, weights, momentum, pos, dct,
    sib_acts, part, hop, plus, minus, hop2, plus2, minus2, cross, cross_in,
    mask, sent, sib_in, pair, pair_in, gathered, total, far_keys,
    load_sems, send_sems, recv_sems,
):
    rep, fsdp = lax.axis_index("rep"), lax.axis_index("fsdp")
    x, zh, y = fsdp // 8, (fsdp // 4) % 2, fsdp % 4
    zl, core = rep // 2, rep % 2
    z = zh * 4 + zl
    other = 1 - zh

    def device(dx=0, dy=0, dz=0, flip=False):
        nz = (z + 8 + dz) % 8
        return (
            (nz % 4) * 2 + ((1 - core) if flip else core),
            ((x + 4 + dx) % 4) * 8 + (nz // 4) * 4 + (y + 4 + dy) % 4,
        )

    def along(axis, step):
        return device(dx=step) if axis == 0 else device(dy=step)

    peers = [along(axis, step) for axis in range(2) for step in (1, 2, 3)]
    peers += [device(dz=d) for d in range(1, 8)] + [device(flip=True)]
    barrier = pltpu.get_barrier_semaphore()
    for peer in peers:
        pl.semaphore_signal(barrier, inc=1, device_id=peer, device_id_type=MESH)

    loads = []

    def load(src, dst):
        copy = pltpu.make_async_copy(src, dst, load_sems.at[len(loads)])
        loads.append(copy)
        copy.start()
        return copy

    def columns(half, step):
        return pl.ds(pl.multiple_of((((x + step) % 4) * 2 + half) * 640, 128), 640)

    order = [(turn, step) for turn in range(2) for step in (2, 1, 3, 0)]
    halves = (other, zh)
    cots_load = load(cots_in, cots)
    acts_loads = {}
    for turn, step in order:
        lanes = columns(halves[turn], step)
        acts_loads[turn, step] = load(acts_in.at[:, lanes], acts.at[:, lanes])
    small_loads = [load(pos_in, pos), load(momentum_in, momentum), load(weights_in, weights), load(dct_in, dct)]

    copies = []

    class push:
        def __init__(self, src, dst, target):
            slot = len(copies)
            copies.append(self)
            self.copy = pltpu.make_async_remote_copy(
                src_ref=src, dst_ref=dst, send_sem=send_sems.at[slot], recv_sem=recv_sems.at[slot],
                device_id=target, device_id_type=MESH,
            )
            self.arrived = False
            self.copy.start()

        def wait_recv(self):
            if not self.arrived:
                self.copy.wait_recv()
            self.arrived = True

    def finish():
        for copy in copies:
            copy.wait_recv()
        for copy in copies:
            copy.copy.wait_send()

    place = {2: 0, 1: 1, 3: 2, 0: 3}

    def multiply(c, turn, step):
        if c == 0:
            acts_loads[turn, step].wait()
        out = lax.dot_general(
            acts[:, columns(halves[turn], step)], cots[:, c * WIDE : c * WIDE + WIDE],
            (((0,), (0,)), ((), ())), preferred_element_type=F32,
        ).astype(BF)
        for uy in range(4):
            part[c, 0, turn, place[step], uy] = out[uy * 160 : uy * 160 + 80]
            part[c, 1, turn, uy, place[step]] = out[uy * 160 + 80 : uy * 160 + 160]

    def spot(axis, step):
        return place[step] if axis == 0 else (y + step) % 4

    def add(ref, value):
        ref[...] = (ref[...].astype(F32) + value.astype(F32)).astype(BF)

    class Ring:
        def __init__(self, axis, block, first, up, down):
            self.axis, self.block, self.first, self.up, self.down = axis, block, first, up, down

        def up1(self):
            self.u1 = push(self.block(2, 0), self.first(0), along(self.axis, 1))

        def down1(self):
            self.d1 = push(self.block(2, 1), self.first(1), along(self.axis, -1))

        def up2(self):
            self.u2 = push(self.block(1, 1), self.up(1), along(self.axis, 1))

        def down2(self):
            self.d2 = push(self.block(3, 0), self.down(0), along(self.axis, -1))

        def open(self):
            self.up1()
            self.down1()
            self.up2()
            self.down2()

        def relay(self):
            self.u1.wait_recv()
            add(self.block(1, 0), self.first(0)[...])
            self.u3 = push(self.block(1, 0), self.up(0), along(self.axis, 1))
            self.d1.wait_recv()
            add(self.block(3, 1), self.first(1)[...])
            self.d3 = push(self.block(3, 1), self.down(1), along(self.axis, -1))

        def arrive(self):
            for copy in (self.u2, self.d2, self.u3, self.d3):
                copy.wait_recv()

        def direct(self):
            self.straight = [
                push(self.block(step, h), into(h), along(self.axis, step))
                for step, into in ((2, self.first), (1, self.up), (3, self.down))
                for h in range(2)
            ]

        def arrive_direct(self):
            for copy in self.straight:
                copy.wait_recv()

    def first_ring(c, s, turn):
        return Ring(
            s,
            lambda step, h: part.at[c, s, turn, spot(s, step), pl.ds(2 * h, 2)],
            lambda h: hop.at[c, s, turn, h],
            lambda h: plus.at[c, s, turn, pl.ds(2 * h, 2)],
            lambda h: minus.at[c, s, turn, pl.ds(2 * h, 2)],
        )

    def second_ring(c, s, turn):
        return Ring(
            1 - s,
            lambda step, h: part.at[c, s, turn, spot(s, 0), spot(1 - s, step), :, pl.ds(256 * h, 256)],
            lambda h: hop2.at[c, s, turn, h],
            lambda h: plus2.at[c, s, turn, h],
            lambda h: minus2.at[c, s, turn, h],
        )

    both = range(2)
    firsts = [[[first_ring(c, s, turn) for s in both] for turn in both] for c in both]
    seconds = [[[second_ring(c, s, turn) for s in both] for turn in both] for c in both]

    def close(c, turn):
        for s in both:
            firsts[c][turn][s].arrive()
            ref = part.at[c, s, turn, spot(s, 0)]
            ref[...] = (
                ref[...].astype(F32) + plus[c, s, turn].astype(F32) + minus[c, s, turn].astype(F32)
            ).astype(BF)
            if (c, turn) == (1, 1):
                seconds[c][turn][s].direct()
            else:
                seconds[c][turn][s].open()

    def relay(rings):
        for ring in rings:
            ring.relay()

    def summed(c, s, turn, h):
        value = (
            part[c, s, turn, spot(s, 0), spot(1 - s, 0), :, h * 256 : h * 256 + 256].astype(F32)
            + plus2[c, s, turn, h].astype(F32)
            + minus2[c, s, turn, h].astype(F32)
        )
        return value + hop2[c, s, turn, h].astype(F32) if (c, turn) == (1, 1) else value

    crossing = [[None, None], [None, None]]

    def cross_over(c):
        for s in both:
            seconds[c][0][s].arrive()
            for h in both:
                cross[c, s, :, h * 256 : h * 256 + 256] = summed(c, s, 0, h).astype(BF)
            crossing[c][s] = push(cross.at[c, s], cross_in.at[c, s], device(dz=4))

    sib_copies = [None, None]

    def decode(c):
        for s in both:
            if c == 1:
                seconds[c][1][s].arrive_direct()
            else:
                seconds[c][1][s].arrive()
            crossing[c][s].wait_recv()
            rows = slice(s * 80, s * 80 + 80)
            for h in both:
                cols = slice(c * WIDE + h * 256, c * WIDE + h * 256 + 256)
                grad = summed(c, s, 1, h) + cross_in[c, s, :, h * 256 : h * 256 + 256].astype(F32)
                moment = 0.9 * momentum[rows, cols] + grad
                sparse = dot3(moment, dct[0], dct[1]) * mask[rows, cols]
                decoded = dot3(sparse, dct[2], dct[3])
                new_mom[rows, cols] = moment - decoded
                decoded = decoded.astype(BF)
                sent[c, h, s] = decoded[:, :128]
                sent[c, h, 2 + s] = decoded[:, 128:]
        sib_copies[c] = push(sent.at[c, 1 - core], sib_in.at[c], device(flip=True))

    pair_copies = [[], []]

    def exchange(c):
        sib_copies[c].wait_recv()
        pair[c] = (sent[c, core].astype(F32) + sib_in[c].astype(F32)).astype(BF)
        for d in range(1, 4):
            peer = (zl + d) % 4
            pair_copies[c].append(push(pair.at[c, peer], pair_in.at[c, d - 1], (peer * 2 + core, fsdp)))

    own = 2 * x + zh
    s_me, j_me = zl % 2, zl // 2
    lanes_me = pl.ds(pl.multiple_of(j_me * 128, 128), 128)
    rows_me = pl.ds(pl.multiple_of(s_me * 80, 16), 80)
    spread = [[], []]

    def half_of(c):
        return pl.ds(pl.multiple_of(c * WIDE + core * 256, 256), 256)

    def renew(c):
        for copy in pair_copies[c]:
            copy.wait_recv()
        update = pair[c, zl].astype(F32)
        for d in range(3):
            update = update + pair_in[c, d].astype(F32)
        old = weights[rows_me, pl.ds(pl.multiple_of(c * WIDE + core * 256 + j_me * 128, 128), 128)]
        gathered[c, own, y, s_me, :, lanes_me] = (old.astype(F32) - (0.03 / 8) * update).astype(BF)
        block = gathered.at[c, own, y, s_me, :, lanes_me]
        for d in (4, 3, 5, 2, 6, 1, 7):
            spread[c].append(push(block, block, device(dz=d)))

    near = [[], []]

    def go_near(c):
        for copy in spread[c]:
            copy.wait_recv()
        for s in both:
            block = gathered.at[c, pl.ds(2 * x, 2), y, s]
            near[c].append([push(block, block, along(s, step)) for step in (2, 1, 3)])
        for s in both:
            new_w[s * 80 : s * 80 + 80, half_of(c)] = gathered[c, own, y, s]
            push(gathered.at[c, own, y, s], new_w.at[pl.ds(s * 80, 80), half_of(c)], device(flip=True))

    far = [[], []]

    def go_far(c):
        for s in both:
            for copy in near[c][s]:
                copy.wait_recv()
            block = gathered.at[c, :, y, s] if s == 0 else gathered.at[c, pl.ds(2 * x, 2), :, s]
            far[c].append([push(block, block, along(1 - s, 1)), push(block, block, along(1 - s, -1))])

    def relay_far(c):
        for s in both:
            for copy in far[c][s]:
                copy.wait_recv()
            spots = []
            for h, step in ((0, 3), (1, 1)):
                if s == 0:
                    spots.append(gathered.at[c, pl.ds(4 * h, 4), (y + step) % 4, s])
                else:
                    spots.append(gathered.at[c, 2 * ((x + step) % 4) + h, :, s])
            far[c][s] = [push(spots[0], spots[0], along(1 - s, 1)), push(spots[1], spots[1], along(1 - s, -1))]

    def terms(c, source, step):
        ux = (x + step) % 4
        rows = gathered[c, pl.ds(2 * ux, 2)].reshape(1280, 256)
        return jnp.dot(
            source[:, pl.ds(pl.multiple_of(ux * 1280, 128), 1280)], rows, preferred_element_type=F32
        )

    def deliver(c, k, value):
        if k == 0:
            far_keys[c] = value.astype(BF)
            push(far_keys.at[c], keys.at[:, half_of(c)], device(flip=True))
        else:
            keys[:, half_of(c)] = value.astype(BF)

    sources = ((0, sib_acts), (1, acts))

    def last_product(c):
        for s in both:
            for copy in far[c][s]:
                copy.wait_recv()
        for k, source in sources:
            total[k] = jnp.zeros((512, 256), F32)

            @pl.loop(0, 4)
            def _(step):
                total[k] += terms(c, source, step)

            deliver(c, k, total[k])

    def far_part(c, step):
        block = gathered.at[c, pl.ds(2 * ((x + step) % 4), 2), y, 0]
        return [push(block, block, along(1, 1)), push(block, block, along(1, -1))]

    def relay_part(c, step, copies):
        for copy in copies:
            copy.wait_recv()
        blocks = [gathered.at[c, 2 * ((x + step) % 4) + h, (y + dy) % 4, 0] for h, dy in ((0, 3), (1, 1))]
        return [push(blocks[0], blocks[0], along(1, 1)), push(blocks[1], blocks[1], along(1, -1))]

    cots_load.wait()
    multiply(0, 0, 2)
    pl.semaphore_wait(barrier, len(peers))
    a0, b0 = firsts[0][0]
    a0.up1()
    a0.down1()
    multiply(0, 0, 1)
    a0.up2()
    b0.up1()
    b0.down2()
    multiply(0, 0, 3)
    a0.down2()
    multiply(0, 0, 0)
    b0.down1()
    b0.up2()
    for step in (2, 1, 3, 0):
        multiply(0, 1, step)
    relay(firsts[0][0])
    for ring in firsts[0][1]:
        ring.open()
    for step in (2, 1, 3, 0):
        multiply(1, 0, step)

    acts_copy = push(acts, sib_acts, device(flip=True))
    for copy in small_loads:
        copy.wait()
    places = pos[...].astype(F32).astype(BF)
    lane = lax.broadcasted_iota(jnp.int32, (128, 1024), 1)
    row = lax.broadcasted_iota(jnp.int32, (128, 1024), 0)
    slot = (lax.broadcasted_iota(jnp.int32, (160, 1024), 1) % 64).astype(F32)
    mask[...] = jnp.zeros_like(mask)
    for t in range(8):
        pick = (row == lane // 64 * 8 + t).astype(F32).astype(BF)
        at = lax.dot_general(places, pick, (((0,), (0,)), ((), ())), preferred_element_type=F32)
        mask[...] += (at == slot).astype(F32)

    close(0, 0)
    relay(firsts[0][1])
    for ring in firsts[1][0]:
        ring.up1()
        ring.down1()
    for step in (2, 1, 3, 0):
        multiply(1, 1, step)
    relay(seconds[0][0])
    close(0, 1)
    for ring in firsts[1][0]:
        ring.up2()
        ring.down2()
    cross_over(0)
    relay(seconds[0][1])
    relay(firsts[1][0])
    for ring in firsts[1][1]:
        ring.open()
    decode(0)
    close(1, 0)
    exchange(0)
    relay(firsts[1][1])
    renew(0)
    relay(seconds[1][0])
    close(1, 1)
    cross_over(1)
    go_near(0)
    decode(1)
    go_far(0)
    exchange(1)
    renew(1)
    acts_copy.wait_recv()
    go_near(1)
    relay_far(0)
    for s in both:
        for copy in near[1][s]:
            copy.wait_recv()
    parts = {step: far_part(1, step) for step in (0, 1, 3)}
    block = gathered.at[1, pl.ds(2 * x, 2), :, 1]
    across = [push(block, block, along(0, 1)), push(block, block, along(0, -1))]
    last_product(0)
    parts[0] = relay_part(1, 0, parts[0])
    parts[2] = far_part(1, 2)
    parts[1] = relay_part(1, 1, parts[1])
    parts[3] = relay_part(1, 3, parts[3])
    for copy in across:
        copy.wait_recv()
    blocks = [gathered.at[1, 2 * ((x + dx) % 4) + h, :, 1] for h, dx in ((0, 3), (1, 1))]
    across = [push(blocks[0], blocks[0], along(0, 1)), push(blocks[1], blocks[1], along(0, -1))]
    parts[2] = relay_part(1, 2, parts[2])
    for step in (0, 1, 3, 2):
        for copy in parts[step] + (across if step == 2 else []):
            copy.wait_recv()
        for k, source in sources:
            if step == 0:
                total[k] = terms(1, source, step)
            elif step != 2:
                total[k] += terms(1, source, step)
            else:
                deliver(1, k, total[k] + terms(1, source, step))
    finish()


def hand_over(*refs):
    sources, targets, held, sems = refs[:3], refs[3:6], refs[6:9], refs[9]
    copies = [pltpu.make_async_copy(sources[i], held[i], sems.at[i]) for i in range(3)]
    for copy in copies:
        copy.start()
    out = []
    for i in range(3):
        copies[i].wait()
        out.append(pltpu.make_async_copy(held[i], targets[i], sems.at[3 + i]))
        out[i].start()
    for copy in out:
        copy.wait()


def on_device(activations, cotangents, weights, momentum, positions):
    vmem = pl.BlockSpec(memory_space=pltpu.VMEM)
    anywhere = pl.BlockSpec(memory_space=pl.ANY)
    pos = positions[0].transpose(1, 2, 0).reshape(128, 160)
    dma = pltpu.SemaphoreType.DMA((N_COPIES,))
    shapes = (
        jax.ShapeDtypeStruct((160, 1024), F32),
        jax.ShapeDtypeStruct((160, 1024), BF),
        jax.ShapeDtypeStruct((512, 1024), BF),
    )
    results = pl.pallas_call(
        kernel,
        name="step",
        out_shape=shapes,
        in_specs=[anywhere] * 6,
        out_specs=(vmem, vmem, vmem),
        scratch_shapes=[
            pltpu.VMEM((512, 5120), BF),
            pltpu.VMEM((512, 1024), BF),
            pltpu.VMEM((160, 1024), BF),
            pltpu.VMEM((160, 1024), F32),
            pltpu.VMEM((128, 160), jnp.int32),
            pltpu.VMEM((4, 256, 256), BF),
            pltpu.VMEM((512, 5120), BF),
            pltpu.VMEM((2, 2, 2, 4, 4, 80, WIDE), BF),
            pltpu.VMEM((2, 2, 2, 2, 2, 80, WIDE), BF),
            pltpu.VMEM((2, 2, 2, 4, 80, WIDE), BF),
            pltpu.VMEM((2, 2, 2, 4, 80, WIDE), BF),
            pltpu.VMEM((2, 2, 2, 2, 80, 256), BF),
            pltpu.VMEM((2, 2, 2, 2, 80, 256), BF),
            pltpu.VMEM((2, 2, 2, 2, 80, 256), BF),
            pltpu.VMEM((2, 2, 80, WIDE), BF),
            pltpu.VMEM((2, 2, 80, WIDE), BF),
            pltpu.VMEM((160, 1024), F32),
            pltpu.VMEM((2, 2, 4, 80, 128), BF),
            pltpu.VMEM((2, 4, 80, 128), BF),
            pltpu.VMEM((2, 4, 80, 128), BF),
            pltpu.VMEM((2, 3, 80, 128), BF),
            pltpu.VMEM((2, 8, 4, 2, 80, 256), BF),
            pltpu.VMEM((2, 512, 256), F32),
            pltpu.VMEM((2, 512, 256), BF),
            pltpu.SemaphoreType.DMA((16,)),
            dma,
            dma,
        ],
        compiler_params=pltpu.CompilerParams(
            collective_id=0, has_side_effects=True, vmem_limit_bytes=60 * 2**20
        ),
    )(activations, cotangents, weights, momentum[0], pos, jnp.asarray(transforms()))
    new_mom, new_w, keys = pl.pallas_call(
        hand_over,
        name="hand_over",
        out_shape=shapes,
        in_specs=[anywhere] * 3,
        out_specs=(anywhere,) * 3,
        scratch_shapes=[pltpu.VMEM(shape.shape, shape.dtype) for shape in shapes]
        + [pltpu.SemaphoreType.DMA((6,))],
        compiler_params=pltpu.CompilerParams(vmem_limit_bytes=60 * 2**20),
    )(*results)
    return new_mom[None], new_w, keys


def solution(mesh):
    placed = (
        P(("rep", "fsdp"), None),
        P(("rep", "fsdp"), None),
        P("fsdp", None),
        P("rep", "fsdp", None),
        P("rep", "fsdp", None, None),
    )
    return jax.shard_map(
        on_device,
        mesh=mesh,
        in_specs=placed,
        out_specs=(P("rep", "fsdp", None), P("fsdp", None), P(("rep", "fsdp"), None)),
        check_vma=False,
    )
```

time: 585 us -> 120 us (0.21)
  waiting for transfers between devices: 429 us -> 0 us
  Pallas kernels: 0 us -> 119 us
  blocking collectives: 68 us -> 0 us
  matrix products: 36 us -> 0 us
  other arithmetic: 27 us -> 0 us
  between operations: 14.1 us -> 0.8 us
  local copies, waits for them, and re-layouts: 11.2 us -> 0 us
    reduce_scatter x1 -> x0, waiting for transfers between devices: 262 us -> none  [on_device(): lax.psum_scatter(lax.dot_general(columns, cotangents, (((0,), (0,)), ((),...]
    all_gather x1 -> x0, waiting for transfers between devices: 166 us -> none  [on_device(): lax.all_gather(new_weights, 'fsdp', axis=0, tiled=True)]
    pallas_call x0 -> x2, Pallas kernels: none -> 119 us  [the longest x1 116 us: on_device(): pl.pallas_call(kernel, name='step', out_shape=shapes, in_specs=[anywhere]...]
    all_gather x2 -> x0, blocking collectives: 68 us -> none  [the longest x1 48.7 us: on_device(): lax.all_gather(kept[None], 'rep', axis=0, tiled=True)]
    dot_general x5 -> x0, matrix products: 36 us -> none  [the longest x1 11.3 us: on_device(): jnp.einsum('rijk,kn->rijn', every_sparse, table, precision=lax.Precision....]
    dot_general x1 -> x0, other arithmetic: 17.5 us -> none  [on_device(): jnp.einsum('rijt,rijtk->rijk', all_kept, every_hot, precision=lax.Precisi...]
    unnamed x8 -> x0, local copies, waits for them, and re-layouts: 8.11 us -> none
  transfers between devices with their start and end apart: 2 -> 0, of which waited for: 2 -> 0; matrix products, arithmetic and copies ran while one was open for 1% -> 0% of each run, Pallas kernels for 0% -> 0%
where the time goes in v2:
time: 120 us; the launch traced here: 119 us
  Pallas kernels  119 us (99%)
    pallas_call x1, Pallas kernels, on_device(): pl.pallas_call(kernel, name='step', out_shape=shapes, in_specs=[anywhere]...  116 us
    pallas_call x1, Pallas kernels, on_device(): pl.pallas_call(hand_over, name='hand_over', out_shape=shapes, in_specs=[a...  2.55 us

profile of v2, /device:TPU:1, one launch (start us, length us, event | category | flops | bytes accessed | tf_op | source)
XLA Modules:
  0.0 119.4 jit_solution(18407246236198624311)
XLA Ops:
  0.6 116.1 %step.1 = (f32[160,1024]{1,0:T(8,128)}, bf16[160,1024]{1,0:T(8,128)(2,1)}, bf16[512,1024]{1,0:T(8,128)(2,1)}) custom-call(bf16[512,5120]{1,0:T(8,128)(2,1)} %acts_in.1, bf16[512,1024]{1,0:T(8,128)(2,1)} %cots_in.1, bf16[160,1024]{1,0:T(8,128)(2,1)} %weights_in.1, f32[160,1024]{1,0:T(8,128)} %bitcast.7, s32[128,160]{1,0:T(8,128)} %bitcast.8, ...), custom_call_target="tpu_custom_call" | custom-call | tf_op jit(solution)/shard_map/step/pallas_call | solution.py:475
  116.7 2.5 %hand_over.1 = (f32[160,1024]{1,0:T(8,128)}, bf16[160,1024]{1,0:T(8,128)(2,1)}, bf16[512,1024]{1,0:T(8,128)(2,1)}) custom-call(f32[160,1024]{1,0:T(8,128)} %get-tuple-element.9.refs_0_, bf16[160,1024]{1,0:T(8,128)(2,1)} %get-tuple-element.10.refs_1_, bf16[512,1024]{1,0:T(8,128)(2,1)} %get-tuple-element.11.refs_2_), custom_call_target="tpu_custom_call" | custom-call | tf_op jit(solution)/shard_map/hand_over/pallas_call | solution.py:514

commit v3 on v2

v3 whole, which is shorter than its diff:
```python
import functools
import math

import jax
import jax.numpy as jnp
import numpy as np
from jax import lax
from jax.experimental import pallas as pl
from jax.experimental.pallas import tpu as pltpu
from jax.sharding import PartitionSpec as P

MESH = pl.DeviceIdType.MESH
BF = jnp.bfloat16
F32 = jnp.float32
N_COPIES = 288
CHUNKS = ((0, 512), (512, 256), (768, 256))
LAST = len(CHUNKS) - 1


def transforms():
    k = np.arange(64, dtype=np.float64)[:, None]
    n = np.arange(64, dtype=np.float64)[None, :]
    table = np.where(k == 0, math.sqrt(1.0 / 64), math.sqrt(2.0 / 64)) * np.cos(math.pi * (2 * n + 1) * k / 128)
    back = np.kron(np.eye(4), table).astype(np.float32)
    high = back.astype(jnp.bfloat16)
    low = (back - high.astype(np.float32)).astype(jnp.bfloat16)
    return np.stack([high.T, low.T, high, low])


def dot3(value, high, low):
    top = value.astype(BF)
    rest = (value - top.astype(F32)).astype(BF)
    dot = functools.partial(jnp.dot, preferred_element_type=F32)
    return dot(top, high) + (dot(rest, high) + dot(top, low))


def kernel(
    acts_in, cots_in, weights_in, momentum_in, pos_in, dct_in,
    new_mom, new_w, keys,
    acts, cots, weights, momentum, pos, dct,
    sib_acts, mask, chunks,
    load_sems, send_sems, recv_sems,
):
    (
        part, hop, plus, minus, hop2, plus2, minus2, cross, cross_in,
        sent, sib_in, pair, pair_in, gathered, total, far_keys,
    ) = zip(*chunks)
    rep, fsdp = lax.axis_index("rep"), lax.axis_index("fsdp")
    x, zh, y = fsdp // 8, (fsdp // 4) % 2, fsdp % 4
    zl, core = rep // 2, rep % 2
    z = zh * 4 + zl
    other = 1 - zh

    def device(dx=0, dy=0, dz=0, flip=False):
        nz = (z + 8 + dz) % 8
        return (
            (nz % 4) * 2 + ((1 - core) if flip else core),
            ((x + 4 + dx) % 4) * 8 + (nz // 4) * 4 + (y + 4 + dy) % 4,
        )

    def along(axis, step):
        return device(dx=step) if axis == 0 else device(dy=step)

    peers = [along(axis, step) for axis in range(2) for step in (1, 2, 3)]
    peers += [device(dz=d) for d in range(1, 8)] + [device(flip=True)]
    loads = []

    def load(src, dst):
        copy = pltpu.make_async_copy(src, dst, load_sems.at[len(loads)])
        loads.append(copy)
        copy.start()
        return copy

    def columns(half, step):
        return pl.ds(pl.multiple_of((((x + step) % 4) * 2 + half) * 640, 128), 640)

    order = [(turn, step) for turn in range(2) for step in (2, 1, 3, 0)]
    halves = (other, zh)
    cots_loads = [load(cots_in.at[:, :512], cots.at[:, :512])]
    acts_loads = {}
    lanes = columns(halves[0], 2)
    acts_loads[0, 2] = load(acts_in.at[:, lanes], acts.at[:, lanes])

    barrier = pltpu.get_barrier_semaphore()
    for peer in peers:
        pl.semaphore_signal(barrier, inc=1, device_id=peer, device_id_type=MESH)

    for turn, step in order[1:]:
        lanes = columns(halves[turn], step)
        acts_loads[turn, step] = load(acts_in.at[:, lanes], acts.at[:, lanes])
    cots_loads.append(load(cots_in.at[:, 512:], cots.at[:, 512:]))
    small_loads = [load(pos_in, pos), load(momentum_in, momentum), load(weights_in, weights), load(dct_in, dct)]

    copies = []

    class push:
        def __init__(self, src, dst, target, when=None, got=None):
            slot = len(copies)
            copies.append(self)
            self.copy = pltpu.make_async_remote_copy(
                src_ref=src, dst_ref=dst, send_sem=send_sems.at[slot], recv_sem=recv_sems.at[slot],
                device_id=target, device_id_type=MESH,
            )
            self.arrived, self.when, self.got = False, when, got
            self.guard(when, self.copy.start)

        def guard(self, condition, act):
            if condition is None:
                act()
            else:
                pl.when(condition)(act)

        def wait_recv(self):
            if not self.arrived:
                self.guard(self.got, self.copy.wait_recv)
            self.arrived = True

        def wait_send(self):
            self.guard(self.when, self.copy.wait_send)

    def finish():
        for copy in copies:
            copy.wait_recv()
        for copy in copies:
            copy.wait_send()

    place = {2: 0, 1: 1, 3: 2, 0: 3}

    def multiply(some, turn, step, at=None):
        first, width = CHUNKS[some[0]][0], sum(CHUNKS[c][1] for c in some)
        out = lax.dot_general(
            acts[:, columns(halves[turn], step)], cots[:, first : first + width],
            (((0,), (0,)), ((), ())), preferred_element_type=F32,
        ).astype(BF)
        at = place[step] if at is None else at
        for c in some:
            cols = slice(CHUNKS[c][0] - first, CHUNKS[c][0] - first + CHUNKS[c][1])
            for uy in range(4):
                part[c][0, turn, at, uy] = out[uy * 160 : uy * 160 + 80, cols]
                part[c][1, turn, uy, at] = out[uy * 160 + 80 : uy * 160 + 160, cols]

    def multiply_all(some, turn):
        @pl.loop(0, 4)
        def _(k):
            multiply(some, turn, (2 - k + 3 * (k // 2) + 2 * (k // 3)) % 4, k)

    def spot(axis, step):
        return place[step] if axis == 0 else (y + step) % 4

    def add(ref, *terms):
        def tile(ref, terms):
            @pl.loop(0, ref.shape[0] // 16)
            def _(k):
                rows = pl.ds(pl.multiple_of(k * 16, 16), 16)
                value = ref[rows].astype(F32)
                for term in terms:
                    value = value + term[rows].astype(F32)
                ref[rows] = value.astype(BF)

        if len(ref.shape) == 2:
            tile(ref, terms)
        else:
            pl.loop(0, ref.shape[0])(lambda i: tile(ref.at[i], [term.at[i] for term in terms]))

    class Ring:
        def __init__(self, axis, block, first, up, down):
            self.axis, self.block, self.first, self.up, self.down = axis, block, first, up, down

        def up1(self):
            self.u1 = push(self.block(2, 0), self.first(0), along(self.axis, 1))

        def down1(self):
            self.d1 = push(self.block(2, 1), self.first(1), along(self.axis, -1))

        def up2(self):
            self.u2 = push(self.block(1, 1), self.up(1), along(self.axis, 1))

        def down2(self):
            self.d2 = push(self.block(3, 0), self.down(0), along(self.axis, -1))

        def open(self):
            self.up1()
            self.down1()
            self.up2()
            self.down2()

        def up3(self):
            self.u1.wait_recv()
            add(self.block(1, 0), self.first(0))
            self.u3 = push(self.block(1, 0), self.up(0), along(self.axis, 1))

        def down3(self):
            self.d1.wait_recv()
            add(self.block(3, 1), self.first(1))
            self.d3 = push(self.block(3, 1), self.down(1), along(self.axis, -1))

        def arrive(self):
            for copy in (self.u2, self.d2, self.u3, self.d3):
                copy.wait_recv()

        def relay(self):
            self.up3()
            self.down3()

    both = range(2)

    def half_cols(c, h):
        half = CHUNKS[c][1] // 2
        return pl.ds(h * half, half)

    def first_ring(c, s, turn):
        return Ring(
            s,
            lambda step, h: part[c].at[s, turn, spot(s, step), pl.ds(2 * h, 2)],
            lambda h: hop[c].at[s, turn, h],
            lambda h: plus[c].at[s, turn, pl.ds(2 * h, 2)],
            lambda h: minus[c].at[s, turn, pl.ds(2 * h, 2)],
        )

    def second_ring(c, s, turn):
        return Ring(
            1 - s,
            lambda step, h: part[c].at[s, turn, spot(s, 0), spot(1 - s, step), :, half_cols(c, h)],
            lambda h: hop2[c].at[s, turn, h],
            lambda h: plus2[c].at[s, turn, h],
            lambda h: minus2[c].at[s, turn, h],
        )

    firsts = [[[first_ring(c, s, turn) for s in both] for turn in both] for c in range(len(CHUNKS))]
    seconds = [[[second_ring(c, s, turn) for s in both] for turn in both] for c in range(len(CHUNKS))]

    def close(c, turn, s):
        firsts[c][turn][s].arrive()
        add(part[c].at[s, turn, spot(s, 0)], plus[c].at[s, turn], minus[c].at[s, turn])
        seconds[c][turn][s].open()

    def summed(c, s, turn, h):
        return (
            part[c][s, turn, spot(s, 0), spot(1 - s, 0), :, half_cols(c, h)].astype(F32)
            + plus2[c][s, turn, h].astype(F32)
            + minus2[c][s, turn, h].astype(F32)
        )

    crossing = [[None, None] for _ in CHUNKS]

    def cross_over(c, s):
        seconds[c][0][s].arrive()
        for h in both:
            cross[c][s, :, half_cols(c, h)] = summed(c, s, 0, h).astype(BF)
        crossing[c][s] = push(cross[c].at[s], cross_in[c].at[s], device(dz=4))

    sib_copies = [None for _ in CHUNKS]

    def decode(c, s):
        seconds[c][1][s].arrive()
        crossing[c][s].wait_recv()
        rows = slice(s * 80, s * 80 + 80)
        for h in both:
            half = CHUNKS[c][1] // 2
            cols = pl.ds(CHUNKS[c][0] + h * half, half)
            grad = summed(c, s, 1, h) + cross_in[c][s, :, half_cols(c, h)].astype(F32)
            moment = 0.9 * momentum[rows, cols] + grad
            table = [dct[i, :half, :half] for i in range(4)]
            sparse = dot3(moment, table[0], table[1]) * mask[rows, cols]
            decoded = dot3(sparse, table[2], table[3])
            new_mom[rows, cols] = moment - decoded
            decoded = decoded.astype(BF)
            for j in range(half // 128):
                sent[c][h, 2 * j + s] = decoded[:, j * 128 : j * 128 + 128]
        if s == 1:
            sib_copies[c] = push(sent[c].at[1 - core], sib_in[c], device(flip=True))

    pair_copies = [[] for _ in CHUNKS]

    def on_duty(c, at):
        return None if CHUNKS[c][1] == 512 else (at + 4) % 4 // 2 == c - 1

    def unit(c, at):
        return at if CHUNKS[c][1] == 512 else at % 2

    def exchange(c):
        sib_copies[c].wait_recv()
        pair[c][...] = (sent[c][core].astype(F32) + sib_in[c][...].astype(F32)).astype(BF)
        for d in range(1, 4):
            peer = (zl + d) % 4
            pair_copies[c].append(
                push(
                    pair[c].at[unit(c, peer)], pair_in[c].at[d - 1], (peer * 2 + core, fsdp),
                    when=on_duty(c, peer), got=on_duty(c, zl),
                )
            )

    own = 2 * x + zh
    s_me, j_me = zl % 2, zl // 2
    rows_me = pl.ds(pl.multiple_of(s_me * 80, 16), 80)
    spread = [[] for _ in CHUNKS]

    def half_of(c):
        first, width = CHUNKS[c]
        return pl.ds(pl.multiple_of(first + core * (width // 2), 128), width // 2)

    def renew(c):
        first, width = CHUNKS[c]
        j = j_me if width == 512 else 0
        lanes_me = pl.ds(pl.multiple_of(j * 128, 128), 128)
        block = gathered[c].at[own, y, s_me, :, lanes_me]
        for copy in pair_copies[c]:
            copy.wait_recv()

        def make():
            update = pair[c][unit(c, zl)].astype(F32)
            for d in range(3):
                update = update + pair_in[c][d].astype(F32)
            old = weights[rows_me, pl.ds(pl.multiple_of(first + core * (width // 2) + j * 128, 128), 128)]
            block[...] = (old.astype(F32) - (0.03 / 8) * update).astype(BF)

        duty = on_duty(c, zl)
        if duty is None:
            make()
        else:
            pl.when(duty)(make)
        for d in (4, 3, 5, 2, 6, 1, 7):
            spread[c].append(push(block, block, device(dz=d), when=duty, got=on_duty(c, zl + 4 - d % 4)))

    near, far, onward = ([[None, None] for _ in CHUNKS] for _ in range(3))

    def go_near(c, s):
        for copy in spread[c]:
            copy.wait_recv()
        block = gathered[c].at[pl.ds(2 * x, 2), y, s]
        near[c][s] = [push(block, block, along(s, step)) for step in (2, 1, 3)]
        new_w[s * 80 : s * 80 + 80, half_of(c)] = gathered[c][own, y, s]
        push(gathered[c].at[own, y, s], new_w.at[pl.ds(s * 80, 80), half_of(c)], device(flip=True))

    def go_far(c, s):
        for copy in near[c][s]:
            copy.wait_recv()
        block = gathered[c].at[:, y, s] if s == 0 else gathered[c].at[pl.ds(2 * x, 2), :, s]
        far[c][s] = [push(block, block, along(1 - s, 1)), push(block, block, along(1 - s, -1))]

    def relay_far(c, s):
        for copy in far[c][s]:
            copy.wait_recv()
        spots = []
        for h, step in ((0, 3), (1, 1)):
            if s == 0:
                spots.append(gathered[c].at[pl.ds(4 * h, 4), (y + step) % 4, s])
            else:
                spots.append(gathered[c].at[2 * ((x + step) % 4) + h, :, s])
        onward[c][s] = [push(spots[0], spots[0], along(1 - s, 1)), push(spots[1], spots[1], along(1 - s, -1))]

    def terms(some, source, step):
        ux = (x + step) % 4
        rows = [gathered[c][pl.ds(2 * ux, 2)].reshape(1280, CHUNKS[c][1] // 2) for c in some]
        rows = jnp.concatenate(rows, axis=1) if len(rows) > 1 else rows[0]
        return jnp.dot(
            source[:, pl.ds(pl.multiple_of(ux * 1280, 128), 1280)], rows, preferred_element_type=F32
        )

    def deliver(c, k, value):
        if k == 0:
            far_keys[c][...] = value.astype(BF)
            push(far_keys[c], keys.at[:, half_of(c)], device(flip=True))
        else:
            keys[:, half_of(c)] = value.astype(BF)

    sources = ((0, sib_acts), (1, acts))

    def last_product(c):
        acts_copy.wait_recv()
        for s in both:
            for copy in onward[c][s]:
                copy.wait_recv()
        for k, source in sources:
            total[c][k] = jnp.zeros(total[c].shape[1:], F32)

            @pl.loop(0, 4)
            def _(step):
                total[c][k] += terms((c,), source, step)

            deliver(c, k, total[c][k])

    def far_part(c, step):
        block = gathered[c].at[pl.ds(2 * ((x + step) % 4), 2), y, 0]
        return [push(block, block, along(1, 1)), push(block, block, along(1, -1))]

    def relay_part(c, step, copies):
        for copy in copies:
            copy.wait_recv()
        blocks = [gathered[c].at[2 * ((x + step) % 4) + h, (y + dy) % 4, 0] for h, dy in ((0, 3), (1, 1))]
        return [push(blocks[0], blocks[0], along(1, 1)), push(blocks[1], blocks[1], along(1, -1))]

    parts, across = {}, []

    def go_last():
        for s in both:
            for copy in near[LAST][s]:
                copy.wait_recv()
        for step in (0, 1, 3):
            parts[step] = far_part(LAST, step)
        block = gathered[LAST].at[pl.ds(2 * x, 2), :, 1]
        across.extend([push(block, block, along(0, 1)), push(block, block, along(0, -1))])

    def relay_last():
        parts[0] = relay_part(LAST, 0, parts[0])
        parts[2] = far_part(LAST, 2)
        parts[1] = relay_part(LAST, 1, parts[1])
        parts[3] = relay_part(LAST, 3, parts[3])
        for copy in across:
            copy.wait_recv()
        blocks = [gathered[LAST].at[2 * ((x + dx) % 4) + h, :, 1] for h, dx in ((0, 3), (1, 1))]
        across.extend([push(blocks[0], blocks[0], along(0, 1)), push(blocks[1], blocks[1], along(0, -1))])
        parts[2] = relay_part(LAST, 2, parts[2])

    cots_loads[0].wait()
    acts_loads[0, 2].wait()
    multiply((0,), 0, 2)
    pl.semaphore_wait(barrier, len(peers))
    a0, b0 = firsts[0][0]
    a0.up1()
    a0.down1()
    acts_loads[0, 1].wait()
    multiply((0,), 0, 1)
    a0.up2()
    b0.up1()
    b0.down2()
    acts_loads[0, 3].wait()
    multiply((0,), 0, 3)
    a0.down2()
    acts_loads[0, 0].wait()
    multiply((0,), 0, 0)
    b0.down1()
    b0.up2()
    for step in (2, 1, 3, 0):
        acts_loads[1, step].wait()
    cots_loads[1].wait()

    multiply_all((0,), 1)
    acts_copy = push(acts, sib_acts, device(flip=True))
    for copy in small_loads:
        copy.wait()
    places = pos[...].astype(F32).astype(BF)
    lane = lax.broadcasted_iota(jnp.int32, (128, 1024), 1)
    row = lax.broadcasted_iota(jnp.int32, (128, 1024), 0)
    slot = (lax.broadcasted_iota(jnp.int32, (160, 1024), 1) % 64).astype(F32)
    mask[...] = jnp.zeros_like(mask)

    @pl.loop(0, 8)
    def _(t):
        pick = (row == lane // 64 * 8 + t).astype(F32).astype(BF)
        at = lax.dot_general(places, pick, (((0,), (0,)), ((), ())), preferred_element_type=F32)
        mask[...] += (at == slot).astype(F32)

    firsts[0][1][0].up1()
    firsts[0][1][0].down1()
    firsts[0][1][1].up1()
    firsts[0][1][1].down1()
    multiply_all((1, 2), 0)
    firsts[0][0][0].up3()
    firsts[0][0][0].down3()
    firsts[0][0][1].up3()
    firsts[0][0][1].down3()
    multiply_all((1, 2), 1)
    firsts[0][1][0].up2()
    firsts[0][1][0].down2()
    firsts[0][1][1].up2()
    firsts[0][1][1].down2()
    firsts[0][1][0].up3()
    firsts[0][1][0].down3()
    firsts[0][1][1].up3()
    firsts[0][1][1].down3()
    close(0, 0, 0)
    close(0, 0, 1)
    firsts[1][0][0].up1()
    firsts[1][0][0].down1()
    firsts[1][0][1].up1()
    firsts[1][0][1].down1()
    firsts[1][0][0].up2()
    firsts[1][0][0].down2()
    firsts[1][0][1].up2()
    firsts[1][0][1].down2()
    close(0, 1, 0)
    close(0, 1, 1)
    seconds[0][0][1].relay()
    seconds[0][0][0].relay()
    firsts[1][0][0].up3()
    firsts[1][0][0].down3()
    firsts[1][0][1].up3()
    firsts[1][0][1].down3()
    firsts[1][1][0].up1()
    firsts[1][1][0].down1()
    firsts[1][1][1].up1()
    firsts[1][1][1].down1()
    seconds[0][1][1].relay()
    seconds[0][1][0].relay()
    cross_over(0, 1)
    firsts[1][1][0].up2()
    firsts[1][1][0].down2()
    firsts[1][1][1].up2()
    cross_over(0, 0)
    firsts[1][1][1].down2()
    firsts[2][0][0].up1()
    close(1, 0, 0)
    close(1, 0, 1)
    firsts[2][0][0].down1()
    firsts[2][0][1].up1()
    firsts[2][0][1].down1()
    firsts[1][1][0].up3()
    firsts[1][1][0].down3()
    firsts[1][1][1].up3()
    firsts[1][1][1].down3()
    firsts[2][0][0].up2()
    firsts[2][0][0].down2()
    firsts[2][0][1].up2()
    firsts[2][0][1].down2()
    seconds[1][0][0].relay()
    firsts[2][1][0].up1()
    firsts[2][0][0].up3()
    firsts[2][1][0].down1()
    seconds[1][0][1].relay()
    firsts[2][1][1].up1()
    firsts[2][1][1].down1()
    firsts[2][0][0].down3()
    firsts[2][0][1].up3()
    decode(0, 0)
    close(1, 1, 0)
    close(1, 1, 1)
    decode(0, 1)
    cross_over(1, 0)
    firsts[2][0][1].down3()
    firsts[2][1][0].up2()
    firsts[2][1][0].down2()
    firsts[2][1][1].up2()
    firsts[2][1][1].down2()
    firsts[2][1][0].up3()
    firsts[2][1][0].down3()
    firsts[2][1][1].up3()
    firsts[2][1][1].down3()
    exchange(0)
    cross_over(1, 1)
    close(2, 0, 0)
    seconds[1][1][1].relay()
    seconds[1][1][0].relay()
    close(2, 0, 1)
    renew(0)
    close(2, 1, 0)
    close(2, 1, 1)
    seconds[2][0][0].relay()
    seconds[2][0][1].relay()
    decode(1, 0)
    decode(1, 1)
    seconds[2][1][0].relay()
    seconds[2][1][1].relay()
    cross_over(2, 0)
    cross_over(2, 1)
    exchange(1)
    go_near(0, 0)
    go_near(0, 1)
    decode(2, 0)
    decode(2, 1)
    renew(1)
    go_far(0, 0)
    go_far(0, 1)
    exchange(2)
    go_near(1, 0)
    go_near(1, 1)
    renew(2)
    relay_far(0, 0)
    relay_far(0, 1)
    go_near(2, 0)
    go_near(2, 1)
    go_far(1, 0)
    go_far(1, 1)
    go_last()
    last_product(0)
    relay_far(1, 0)
    relay_far(1, 1)
    relay_last()

    for s in both:
        for copy in onward[1][s]:
            copy.wait_recv()
    for step in (0, 1, 3, 2):
        for copy in parts[step] + (across if step == 2 else []):
            copy.wait_recv()
        for k, source in sources:
            value = terms((1, 2), source, step)
            if step == 0:
                total[0][k] = value
            elif step != 2:
                total[0][k] += value
            else:
                value = total[0][k] + value
                deliver(1, k, value[:, :128])
                deliver(2, k, value[:, 128:])
    finish()


def hand_over(*refs):
    copies = [pltpu.make_async_copy(refs[i], refs[3 + i], refs[6].at[i]) for i in range(3)]
    for copy in copies:
        copy.start()
    for copy in copies:
        copy.wait()


def chunk_scratch(width):
    half = width // 2
    units = 2 * half // 128
    shapes = [
        (2, 2, 4, 4, 80, width),
        (2, 2, 2, 2, 80, width),
        (2, 2, 4, 80, width),
        (2, 2, 4, 80, width),
        (2, 2, 2, 80, half),
        (2, 2, 2, 80, half),
        (2, 2, 2, 80, half),
        (2, 80, width),
        (2, 80, width),
        (2, units, 80, 128),
        (units, 80, 128),
        (units, 80, 128),
        (3, 80, 128),
        (8, 4, 2, 80, half),
    ]
    held = [pltpu.VMEM(shape, BF) for shape in shapes]
    return (*held, pltpu.VMEM((2, 512, half), F32), pltpu.VMEM((512, half), BF))


def on_device(activations, cotangents, weights, momentum, positions):
    vmem = pl.BlockSpec(memory_space=pltpu.VMEM)
    anywhere = pl.BlockSpec(memory_space=pl.ANY)
    pos = positions[0].transpose(1, 2, 0).reshape(128, 160)
    dma = pltpu.SemaphoreType.DMA((N_COPIES,))
    shapes = (
        jax.ShapeDtypeStruct((160, 1024), F32),
        jax.ShapeDtypeStruct((160, 1024), BF),
        jax.ShapeDtypeStruct((512, 1024), BF),
    )
    results = pl.pallas_call(
        kernel,
        name="step",
        out_shape=tuple(pltpu.VMEM(shape.shape, shape.dtype) for shape in shapes),
        in_specs=[anywhere] * 6,
        out_specs=(vmem, vmem, vmem),
        scratch_shapes=[
            pltpu.VMEM((512, 5120), BF),
            pltpu.VMEM((512, 1024), BF),
            pltpu.VMEM((160, 1024), BF),
            pltpu.VMEM((160, 1024), F32),
            pltpu.VMEM((128, 160), jnp.int32),
            pltpu.VMEM((4, 256, 256), BF),
            pltpu.VMEM((512, 5120), BF),
            pltpu.VMEM((160, 1024), F32),
            [chunk_scratch(width) for first, width in CHUNKS],
            pltpu.SemaphoreType.DMA((16,)),
            dma,
            dma,
        ],
        compiler_params=pltpu.CompilerParams(
            collective_id=0, has_side_effects=True, vmem_limit_bytes=61 * 2**20
        ),
    )(activations, cotangents, weights, momentum[0], pos, jnp.asarray(transforms()))
    new_mom, new_w, keys = pl.pallas_call(
        hand_over,
        name="hand_over",
        out_shape=shapes,
        in_specs=[vmem] * 3,
        out_specs=(anywhere,) * 3,
        scratch_shapes=[pltpu.SemaphoreType.DMA((3,))],
        compiler_params=pltpu.CompilerParams(vmem_limit_bytes=4 * 2**20),
    )(*results)
    return new_mom[None], new_w, keys


def solution(mesh):
    placed = (
        P(("rep", "fsdp"), None),
        P(("rep", "fsdp"), None),
        P("fsdp", None),
        P("rep", "fsdp", None),
        P("rep", "fsdp", None, None),
    )
    return jax.shard_map(
        on_device,
        mesh=mesh,
        in_specs=placed,
        out_specs=(P("rep", "fsdp", None), P("fsdp", None), P(("rep", "fsdp"), None)),
        check_vma=False,
    )
```

time: 120 us -> 116 us (0.967)
  Pallas kernels: 119 us -> 115 us
    pallas_call x2, Pallas kernels: 119 us -> 115 us  [the longest x1 113 us: on_device(): pl.pallas_call(kernel, name='step', out_shape=tuple((pltpu.VMEM(shape.sha...]
where the time goes in v3:
time: 116 us; the launch traced here: 115 us
  Pallas kernels  115 us (99%)
    pallas_call x1, Pallas kernels, on_device(): pl.pallas_call(kernel, name='step', out_shape=tuple((pltpu.VMEM(shape.sha...  113 us

profile of v3, /device:TPU:1, one launch (start us, length us, event | category | flops | bytes accessed | tf_op | source)
XLA Modules:
  0.0 115.5 jit_solution(12869588058554399399)
XLA Ops:
  0.6 113.4 %step.1 = (f32[160,1024]{1,0:T(8,128)S(1)}, bf16[160,1024]{1,0:T(8,128)(2,1)S(1)}, bf16[512,1024]{1,0:T(8,128)(2,1)S(1)}) custom-call(bf16[512,5120]{1,0:T(8,128)(2,1)} %acts_in.1, bf16[512,1024]{1,0:T(8,128)(2,1)} %cots_in.1, bf16[160,1024]{1,0:T(8,128)(2,1)} %weights_in.1, f32[160,1024]{1,0:T(8,128)} %bitcast.7, s32[128,160]{1,0:T(8,128)} %bitcast.8, ...), custom_call_target="tpu_custom_call" | custom-call | tf_op jit(solution)/shard_map/step/pallas_call | solution.py:640
  114.0 1.3 %hand_over.1 = (f32[160,1024]{1,0:T(8,128)}, bf16[160,1024]{1,0:T(8,128)(2,1)}, bf16[512,1024]{1,0:T(8,128)(2,1)}) custom-call(f32[160,1024]{1,0:T(8,128)S(1)} %get-tuple-element.9.refs_0_, bf16[160,1024]{1,0:T(8,128)(2,1)S(1)} %get-tuple-element.10.refs_1_, bf16[512,1024]{1,0:T(8,128)(2,1)S(1)} %get-tuple-element.11.refs_2_), custom_call_target="tpu_custom_call" | custom-call | tf_op jit(solution)/shard_map/hand_over/pallas_call | solution.py:664

commit v4 on v3

--- a/solution.py
+++ b/solution.py
@@ -43,7 +43,7 @@
 ):
     (
         part, hop, plus, minus, hop2, plus2, minus2, cross, cross_in,
-        sent, sib_in, pair, pair_in, gathered, total, far_keys,
+        sent, pair_in, gathered, total, far_keys,
     ) = zip(*chunks)
     rep, fsdp = lax.axis_index("rep"), lax.axis_index("fsdp")
     x, zh, y = fsdp // 8, (fsdp // 4) % 2, fsdp % 4
@@ -62,7 +62,7 @@
         return device(dx=step) if axis == 0 else device(dy=step)
 
     peers = [along(axis, step) for axis in range(2) for step in (1, 2, 3)]
-    peers += [device(dz=d) for d in range(1, 8)] + [device(flip=True)]
+    peers += [device(dz=d) for d in range(1, 8)] + [((zl + d) % 4 * 2 + 1 - core, fsdp) for d in range(4)]
     loads = []
 
     def load(src, dst):
@@ -248,8 +248,6 @@
         for h in both:
             cross[c][s, :, half_cols(c, h)] = summed(c, s, 0, h).astype(BF)
         crossing[c][s] = push(cross[c].at[s], cross_in[c].at[s], device(dz=4))
-
-    sib_copies = [None for _ in CHUNKS]
 
     def decode(c, s):
         seconds[c][1][s].arrive()
@@ -268,7 +266,7 @@
             for j in range(half // 128):
                 sent[c][h, 2 * j + s] = decoded[:, j * 128 : j * 128 + 128]
         if s == 1:
-            sib_copies[c] = push(sent[c].at[1 - core], sib_in[c], device(flip=True))
+            exchange(c)
 
     pair_copies = [[] for _ in CHUNKS]
 
@@ -279,16 +277,17 @@
         return at if CHUNKS[c][1] == 512 else at % 2
 
     def exchange(c):
-        sib_copies[c].wait_recv()
-        pair[c][...] = (sent[c][core].astype(F32) + sib_in[c][...].astype(F32)).astype(BF)
-        for d in range(1, 4):
+        for d in range(4):
             peer = (zl + d) % 4
-            pair_copies[c].append(
-                push(
-                    pair[c].at[unit(c, peer)], pair_in[c].at[d - 1], (peer * 2 + core, fsdp),
-                    when=on_duty(c, peer), got=on_duty(c, zl),
-                )
-            )
+            for flip in range(2):
+                if d + flip > 0:
+                    side = (1 - core) if flip else core
+                    pair_copies[c].append(
+                        push(
+                            sent[c].at[side, unit(c, peer)], pair_in[c].at[2 * d + flip - 1],
+                            (peer * 2 + side, fsdp), when=on_duty(c, peer), got=on_duty(c, zl),
+                        )
+                    )
 
     own = 2 * x + zh
     s_me, j_me = zl % 2, zl // 2
@@ -308,8 +307,8 @@
             copy.wait_recv()
 
         def make():
-            update = pair[c][unit(c, zl)].astype(F32)
-            for d in range(3):
+            update = sent[c][core, unit(c, zl)].astype(F32)
+            for d in range(7):
                 update = update + pair_in[c][d].astype(F32)
             old = weights[rows_me, pl.ds(pl.multiple_of(first + core * (width // 2) + j * 128, 128), 128)]
             block[...] = (old.astype(F32) - (0.03 / 8) * update).astype(BF)
@@ -536,7 +535,6 @@
     firsts[2][1][0].down3()
     firsts[2][1][1].up3()
     firsts[2][1][1].down3()
-    exchange(0)
     cross_over(1, 1)
     close(2, 0, 0)
     seconds[1][1][1].relay()
@@ -553,7 +551,6 @@
     seconds[2][1][1].relay()
     cross_over(2, 0)
     cross_over(2, 1)
-    exchange(1)
     go_near(0, 0)
     go_near(0, 1)
     decode(2, 0)
@@ -561,7 +558,6 @@
     renew(1)
     go_far(0, 0)
     go_far(0, 1)
-    exchange(2)
     go_near(1, 0)
     go_near(1, 1)
     renew(2)
@@ -618,9 +614,7 @@
         (2, 80, width),
         (2, 80, width),
         (2, units, 80, 128),
-        (units, 80, 128),
-        (units, 80, 128),
-        (3, 80, 128),
+        (7, 80, 128),
         (8, 4, 2, 80, half),
     ]
     held = [pltpu.VMEM(shape, BF) for shape in shapes]

time: 116 us -> 114 us (0.983)
  Pallas kernels: 115 us -> 113 us
    pallas_call x1, Pallas kernels: 113 us -> 112 us  [on_device(): pl.pallas_call(kernel, name='step', out_shape=tuple((pltpu.VMEM(shape.sha...]
where the time goes in v4:
time: 114 us
  Pallas kernels  113 us (99%)
    pallas_call x1, Pallas kernels, on_device(): pl.pallas_call(kernel, name='step', out_shape=tuple((pltpu.VMEM(shape.sha...  112 us

profile of v4, /device:TPU:1, one launch (start us, length us, event | category | flops | bytes accessed | tf_op | source)
XLA Modules:
  0.0 114.1 jit_solution(15823630158394452662)
XLA Ops:
  0.6 112.0 %step.1 = (f32[160,1024]{1,0:T(8,128)S(1)}, bf16[160,1024]{1,0:T(8,128)(2,1)S(1)}, bf16[512,1024]{1,0:T(8,128)(2,1)S(1)}) custom-call(bf16[512,5120]{1,0:T(8,128)(2,1)} %acts_in.1, bf16[512,1024]{1,0:T(8,128)(2,1)} %cots_in.1, bf16[160,1024]{1,0:T(8,128)(2,1)} %weights_in.1, f32[160,1024]{1,0:T(8,128)} %bitcast.7, s32[128,160]{1,0:T(8,128)} %bitcast.8, ...), custom_call_target="tpu_custom_call" | custom-call | tf_op jit(solution)/shard_map/step/pallas_call | solution.py:634
  112.6 1.3 %hand_over.1 = (f32[160,1024]{1,0:T(8,128)}, bf16[160,1024]{1,0:T(8,128)(2,1)}, bf16[512,1024]{1,0:T(8,128)(2,1)}) custom-call(f32[160,1024]{1,0:T(8,128)S(1)} %get-tuple-element.9.refs_0_, bf16[160,1024]{1,0:T(8,128)(2,1)S(1)} %get-tuple-element.10.refs_1_, bf16[512,1024]{1,0:T(8,128)(2,1)S(1)} %get-tuple-element.11.refs_2_), custom_call_target="tpu_custom_call" | custom-call | tf_op jit(solution)/shard_map/hand_over/pallas_call | solution.py:658
